TPU v7x, 512 devices: a whole 4x4x16 slice. The times are simulated.
512 devices in a mesh: energy: 128 (over z, x, core), slab: 4 (over y).
Axes of the slice: x: 4, y: 4, z: 16, core: 2. Of those that a mesh axis runs over, the one named last changes fastest.
Arguments:
- g0e: bfloat16 [128, 8, 256, 256], P('energy', 'slab'), as said below
- hcoup: bfloat16 [8, 256, 256], P('slab'), may hold values from -0.375 to 0.375
- sigma_in: bfloat16 [128, 8, 256, 256], P('energy', 'slab'), may hold values from -4 to 4
- gph0: bfloat16 [128, 8, 256, 256], P('energy', 'slab'), as said below
- hph: bfloat16 [8, 256, 256], P('slab'), may hold values from -0.375 to 0.375
- pair_lo: int32 [128, 4], replicated, may hold values from 0 to 119
- freq_offset: int32 [128], replicated, may hold values from 1 to 8
- pair_weight: float32 [128, 4], replicated, may hold values from 0.1 to 1
- active: int32 [128], P('energy'), may hold values from 0 to 1, as said below
Outputs:
- sigma_out: bfloat16 [128, 8, 256, 256], P('energy', 'slab')
Inputs may be any that keep to these rules, and one draw needn't show every extreme that they name: active holds whole numbers; the active energies of an index of energy are its first ones. `g0e`: every block is a dominant diagonal plus dense independent entries. `gph0`: every block is a dominant diagonal plus dense independent entries.
All inputs are finite; a program needn't handle non-finite values.
Results may differ from a plain program's by a relative error of at most 0.0082.
Values may be sent and summed in bfloat16 or wider, within the bound.
A program may use at most 64 MiB of HBM per device.

v0:
```python
import jax
import jax.numpy as jnp
from jax import lax
from jax.sharding import PartitionSpec as P

precise = lax.Precision.HIGHEST


def prefix(value, axis, join, neutral):
    count, mine = (lax.axis_size(axis), lax.axis_index(axis))
    pieces = jax.tree.map(lambda part: lax.all_gather(part, axis), value)
    so_far = jax.tree.map(
        lambda part, zero: jnp.full_like(part, 0) + jnp.asarray(zero, part.dtype), value, neutral
    )

    def step(position, so_far):
        longer = join(so_far, jax.tree.map(lambda part: part[position], pieces))
        return jax.tree.map(lambda new, old: jnp.where(position < mine, new, old), longer, so_far)

    return lax.fori_loop(0, count - 1, step, so_far)


def sandwich(outer, inner):
    left = jnp.einsum("...ij,...jk->...ik", outer, inner, precision=precise)
    return jnp.einsum("...ik,...lk->...il", left, outer, precision=precise)


def link_maps(inverse, coupling, source):
    prefix_maps = []
    prefix_sums = []
    for slab_idx in range(inverse.shape[1]):
        block_inv = inverse[:, slab_idx].astype(jnp.float32)
        transfer = jnp.einsum(
            "nij,jk->nik", block_inv, coupling[slab_idx].astype(jnp.float32), precision=precise
        )
        injected = sandwich(block_inv, source[:, slab_idx].astype(jnp.float32))
        if slab_idx == 0:
            new_map = transfer
            new_sum = injected
        else:
            new_map = jnp.einsum("nij,njk->nik", transfer, prefix_maps[-1], precision=precise)
            new_sum = sandwich(transfer, prefix_sums[-1]) + injected
        prefix_maps.append(new_map)
        prefix_sums.append(new_sum)
    return (jnp.stack(prefix_maps, 1), jnp.stack(prefix_sums, 1))


def compose(earlier, later):
    map_early, sum_early = earlier
    map_late, sum_late = later
    joined = jnp.einsum("nij,njk->nik", map_late, map_early, precision=precise)
    return (joined, sandwich(map_late, sum_early) + sum_late)


def per_device(g0e, hcoup, sigma_in, gph0, hph, pair_lo, freq_offset, pair_weight, active):
    groups = lax.axis_size("energy")
    local_energies = g0e.shape[0]
    local_freqs = gph0.shape[0]
    slab_count = g0e.shape[1]
    order = g0e.shape[2]
    piece = order * order // groups
    active_count = active[0]
    top_idx = pair_lo + freq_offset[:, None]
    elec_maps, elec_sums = link_maps(g0e, hcoup, sigma_in)
    keep = (jnp.arange(local_energies, dtype=jnp.int32) < active_count).astype(jnp.float32)
    elec_maps = elec_maps * keep[:, None, None, None]
    elec_sums = elec_sums * keep[:, None, None, None]
    elec_last = (elec_maps[:, -1], elec_sums[:, -1])
    ident_e = (
        jnp.broadcast_to(jnp.eye(order, dtype=jnp.float32), (local_energies, order, order)),
        jnp.zeros((local_energies, order, order), jnp.float32),
    )
    entering = prefix(elec_last, "slab", compose, ident_e)
    elec_in = entering[1]
    electron_green = sandwich(elec_maps, elec_in[:, None]) + elec_sums
    green_send = electron_green.astype(jnp.bfloat16).reshape(
        local_energies, slab_count, groups, piece
    )
    arrived = lax.all_to_all(green_send, "energy", split_axis=2, concat_axis=0, tiled=True)
    bottom = arrived[pair_lo].astype(jnp.float32)
    upper_rows = arrived[top_idx].astype(jnp.float32)
    weights = pair_weight[:, :, None, None, None]
    summed = jnp.sum(weights * bottom * upper_rows, axis=1)
    pol_rows = summed.astype(jnp.bfloat16)
    pol_owned = lax.all_to_all(pol_rows, "energy", split_axis=0, concat_axis=2, tiled=True)
    polarization = pol_owned.reshape(local_freqs, slab_count, order, order)
    phon_maps, phon_sums = link_maps(gph0, hph, polarization)
    phon_last = (phon_maps[:, -1], phon_sums[:, -1])
    ident_p = (
        jnp.broadcast_to(jnp.eye(order, dtype=jnp.float32), (local_freqs, order, order)),
        jnp.zeros((local_freqs, order, order), jnp.float32),
    )
    entering_p = prefix(phon_last, "slab", compose, ident_p)
    phon_in = entering_p[1]
    phonon_green = sandwich(phon_maps, phon_in[:, None]) + phon_sums
    phonon_send = phonon_green.astype(jnp.bfloat16).reshape(local_freqs, slab_count, groups, piece)
    phonon_rows = lax.all_to_all(phonon_send, "energy", split_axis=2, concat_axis=0, tiled=True)
    phonon_float = phonon_rows.astype(jnp.float32)[:, None]
    weights = pair_weight[:, :, None, None, None]
    to_bottom = weights * phonon_float * arrived[top_idx].astype(jnp.float32)
    to_upper = weights * phonon_float * arrived[pair_lo].astype(jnp.float32)
    terms = jnp.concatenate([to_bottom, to_upper], axis=0).reshape(-1, slab_count, 1, piece)
    targets = jnp.concatenate([pair_lo, top_idx], axis=0).reshape(-1)
    sigma_rows = jax.ops.segment_sum(terms, targets, num_segments=arrived.shape[0])
    sigma_owned = lax.all_to_all(
        sigma_rows.astype(jnp.bfloat16), "energy", split_axis=0, concat_axis=2, tiled=True
    )
    return sigma_owned.reshape(local_energies, slab_count, order, order)


def solution(mesh):
    placed = (
        P("energy", "slab", None, None),
        P("slab", None, None),
        P("energy", "slab", None, None),
        P("energy", "slab", None, None),
        P("slab", None, None),
        P(),
        P(),
        P(),
        P("energy"),
    )
    return jax.shard_map(
        per_device,
        mesh=mesh,
        in_specs=placed,
        out_specs=P("energy", "slab", None, None),
        check_vma=False,
    )
```

profile of v0, /device:TPU:24, one launch (start us, length us, event | category | flops | bytes accessed | tf_op | source)
XLA Modules:
  0.0 391.0 jit_solution(14533540448701720249)
XLA Ops:
  6.5 1.2 fusion.43
  7.7 1.1 fusion.41
  8.9 1.2 fusion.52
  10.2 1.2 fusion.45
  11.7 0.4 fusion.92
  13.2 0.7 fusion.33
  14.6 0.7 fusion.34
  15.3 33.7 %all-gather.9.cloned.1.call-done = f32[4,1,256,256]{3,2,1,0:T(8,128)} async-done(((f32[1,1,256,256]{3,2,1,0:T(8,128)}), f32[4,1,256,256]{3,2,1,0:T(8,128)}) %all-gather.9.cloned.1.call-update) | async-done | bytes 1048592 | tf_op jit(solution)/shard_map/all_gather | solution.py:11
  49.0 34.2 %all-gather.7.cloned.1.call-done = f32[4,1,256,256]{3,2,1,0:T(8,128)} async-done(((f32[1,1,256,256]{3,2,1,0:T(8,128)}), f32[4,1,256,256]{3,2,1,0:T(8,128)}) %all-gather.7.cloned.1.call-update) | async-done | bytes 1048592 | tf_op jit(solution)/shard_map/all_gather | solution.py:11
  83.2 8.6 %while.28 = (s32[]{:T(128)}, f32[1,256,256]{2,1,0:T(8,128)S(1)}, s32[]{:T(128)}, f32[4,1,256,256]{3,2,1,0:T(8,128)}, f32[4,1,256,256]{3,2,1,0:T(8,128)}, /*index=5*/s32[]{:T(128)}, s32[]{:T(128)}) while((s32[]{:T(128)}, f32[1,256,256]{2,1,0:T(8,128)S(1)}, s32[]{:T(128)}, f32[4,1,256,256]{3,2,1,0:T(8,128)}, ...), condition=%wide.region_1.2_spmd.clone, body=%wide.region_0.1_spmd.clone.sunk | while | flops 402915328 | bytes 2098786 | solution.py:20
  83.2 1.3 fusion.131
  84.5 1.5 fusion.132
  86.0 1.3 fusion.131
  87.4 1.5 fusion.132
  88.9 1.3 fusion.131
  90.2 1.5 fusion.132
  91.7 0.6 fusion.32
  92.3 0.7 fusion.29
  93.1 1.0 copy.32
  94.1 16.8 %all-to-all-start = ((bf16[1,2,128,512]{3,1,0,2:T(2,128)(2,1)}), bf16[1,2,128,512]{3,1,0,2:T(2,128)(2,1)S(1)}, u32[]{:S(2)}, u32[]{:S(2)}) async-start(bf16[1,2,128,512]{3,1,0,2:T(2,128)(2,1)} %copy.32), calls=%async_computation | async-start | bytes 524288 | tf_op jit(solution)/shard_map/all_to_all | solution.py:79
  111.6 19.5 %all-to-all-done = bf16[1,2,128,512]{3,1,0,2:T(2,128)(2,1)S(1)} async-done(((bf16[1,2,128,512]{3,1,0,2:T(2,128)(2,1)}), bf16[1,2,128,512]{3,1,0,2:T(2,128)(2,1)S(1)}, u32[]{:S(2)}, u32[]{:S(2)}) %all-to-all-start) | async-done | bytes 262176 | tf_op jit(solution)/shard_map/all_to_all | solution.py:79
  131.1 3.6 gather_fusion
  134.7 3.6 gather_fusion.1
  138.2 3.0 fusion.28
  141.2 8.8 %all-to-all-start.1 = ((bf16[128,2,1,512]{3,1,2,0:T(2,128)(2,1)}), bf16[128,2,1,512]{3,1,2,0:T(2,128)(2,1)S(1)}, u32[]{:S(2)}, u32[]{:S(2)}) async-start(bf16[128,2,1,512]{3,1,2,0:T(2,128)(2,1)} %bitcast.152), calls=%async_computation.1 | async-start | bytes 524288 | tf_op jit(solution)/shard_map/all_to_all | solution.py:85
  150.5 1.1 fusion.89
  151.7 18.5 %all-to-all-done.1 = bf16[128,2,1,512]{3,1,2,0:T(2,128)(2,1)S(1)} async-done(((bf16[128,2,1,512]{3,1,2,0:T(2,128)(2,1)}), bf16[128,2,1,512]{3,1,2,0:T(2,128)(2,1)S(1)}, u32[]{:S(2)}, u32[]{:S(2)}) %all-to-all-start.1) | async-done | bytes 262176 | tf_op jit(solution)/shard_map/all_to_all | solution.py:85
  171.5 0.4 fusion.94
  172.0 1.1 convolution_add_fusion.4
  173.1 11.3 %all-gather.11.cloned.1.call-done = f32[1024,256]{1,0:T(8,128)} async-done(((f32[256,256]{1,0:T(8,128)}), f32[1024,256]{1,0:T(8,128)}) %all-gather.11.cloned.1.call-update) | async-done | bytes 1048592 | tf_op jit(solution)/shard_map/all_gather | solution.py:11
  184.4 34.0 %all-gather.13.cloned.1.call-done = f32[1024,256]{1,0:T(8,128)} async-done(((f32[256,256]{1,0:T(8,128)}), f32[1024,256]{1,0:T(8,128)}) %all-gather.13.cloned.1.call-update) | async-done | bytes 1048592 | tf_op jit(solution)/shard_map/all_gather | solution.py:11
  218.4 8.6 %while.29 = (s32[]{:T(128)}, f32[1,256,256]{2,1,0:T(8,128)S(1)}, s32[]{:T(128)}, f32[4,1,256,256]{3,2,1,0:T(8,128)}, f32[4,1,256,256]{3,2,1,0:T(8,128)}, /*index=5*/s32[]{:T(128)}, s32[]{:T(128)}) while((s32[]{:T(128)}, f32[1,256,256]{2,1,0:T(8,128)S(1)}, s32[]{:T(128)}, f32[4,1,256,256]{3,2,1,0:T(8,128)}, ...), condition=%wide.region_4.5_spmd.clone, body=%wide.region_3.4_spmd.clone.sunk | while | flops 402915328 | bytes 2098786 | solution.py:20
  218.4 1.4 fusion.137
  219.8 1.5 fusion.138
  221.3 1.3 fusion.137
  222.6 1.5 fusion.138
  224.1 1.3 fusion.137
  225.5 1.5 fusion.138
  227.0 0.6 fusion.31
  227.6 1.6 fusion.30
  229.3 1.0 copy.39
  230.3 17.1 %all-to-all-start.2 = ((bf16[1,2,128,512]{3,1,0,2:T(2,128)(2,1)}), bf16[1,2,128,512]{3,1,0,2:T(2,128)(2,1)S(1)}, u32[]{:S(2)}, u32[]{:S(2)}) async-start(bf16[1,2,128,512]{3,1,0,2:T(2,128)(2,1)} %copy.39), calls=%async_computation.2 | async-start | bytes 524288 | tf_op jit(solution)/shard_map/all_to_all | solution.py:97
  247.6 19.6 %all-to-all-done.2 = bf16[1,2,128,512]{3,1,0,2:T(2,128)(2,1)S(1)} async-done(((bf16[1,2,128,512]{3,1,0,2:T(2,128)(2,1)}), bf16[1,2,128,512]{3,1,0,2:T(2,128)(2,1)S(1)}, u32[]{:S(2)}, u32[]{:S(2)}) %all-to-all-start.2) | async-done | bytes 262176 | tf_op jit(solution)/shard_map/all_to_all | solution.py:97
  267.4 2.1 multiply_multiply_fusion.1
  269.6 4.1 %pad_maximum_fusion = f32[256,4,2,1,512]{4,2,1,0,3:T(2,128)} fusion(f32[128,4,2,1,512]{4,2,1,0,3:T(2,128)S(1)} %get-tuple-element.274, f32[128,4,2,1,512]{4,2,1,0,3:T(2,128)S(1)} %get-tuple-element.273), kind=kLoop, calls=%fused_computation.33 | loop fusion | flops 1048576 | bytes 8388608 | tf_op jit(solution)/shard_map/concatenate | solution.py:102
  273.8 81.1 %scatter_fusion = f32[128,2,512]{2,1,0:T(2,128)S(1)} fusion(f32[128,2,512]{2,1,0:T(2,128)S(1)} %broadcast.67, s32[1024]{0:T(1024)S(1)} %reshape.390, f32[1024,2,512]{2,1,0:T(2,128)} %bitcast.199), kind=kCustom, calls=%fused_computation.2 | custom fusion | flops 1048576 | bytes 12587008 | tf_op jit(solution)/shard_map/scatter-add | solution.py:104
  355.1 28.6 %all_to_all.57 = bf16[128,2,1,512]{3,1,2,0:T(2,128)(2,1)S(1)} all-to-all(bf16[128,2,1,512]{3,1,2,0:T(2,128)(2,1)S(1)} %convert_bitcast_fusion.1), channel_id=1, replica_groups=mesh['energy'=128,'slab'=4] {'energy'}, dimensions={0} | all-to-all | bytes 524288 | tf_op jit(solution)/shard_map/all_to_all | solution.py:105
  383.7 0.8 reshape.362
  (55 shorter events, 4.7 us)
Async XLA Ops:
  6.5 6.3 %copy-start.1 = (bf16[1,2,256,256]{3,2,1,0:T(8,128)(2,1)S(1)}, bf16[1,2,256,256]{3,2,1,0:T(8,128)(2,1)}, u32[]{:S(2)}) copy-start(bf16[1,2,256,256]{3,2,1,0:T(8,128)(2,1)} %param.13) | copy-start | bytes 786436
  6.5 42.4 %all-gather.9.cloned.1.call-start = ((), (), s32[]{:S(2)}) async-start(), calls=%async_computation.5 | async-start | bytes 1310720 | tf_op jit(solution)/shard_map/all_gather | solution.py:11
  10.2 3.8 copy-start.3
  13.9 69.2 %all-gather.7.cloned.1.call-start = ((), (), s32[]{:S(2)}) async-start(), calls=%async_computation.4 | async-start | bytes 1310720 | tf_op jit(solution)/shard_map/all_gather | solution.py:11
  91.7 19.2 %copy-start.5 = (s32[128,4]{0,1:T(4,128)S(1)}, s32[128,4]{0,1:T(4,128)}, u32[]{:S(2)}) copy-start(s32[128,4]{0,1:T(4,128)} %param.18) | copy-start | bytes 6148
  91.7 19.2 %copy-start.7 = (s32[128]{0:T(128)S(1)}, s32[128]{0:T(128)}, u32[]{:S(2)}) copy-start(s32[128]{0:T(128)} %param.19) | copy-start | bytes 1540
  92.3 19.1 %copy-start.6 = (f32[128,4]{0,1:T(4,128)S(1)}, f32[128,4]{0,1:T(4,128)}, u32[]{:S(2)}) copy-start(f32[128,4]{0,1:T(4,128)} %param.20) | copy-start | bytes 6148
  94.1 37.0 %all-to-all-start = ((bf16[1,2,128,512]{3,1,0,2:T(2,128)(2,1)}), bf16[1,2,128,512]{3,1,0,2:T(2,128)(2,1)S(1)}, u32[]{:S(2)}, u32[]{:S(2)}) async-start(bf16[1,2,128,512]{3,1,0,2:T(2,128)(2,1)} %copy.32), calls=%async_computation | async-start | bytes 524288 | tf_op jit(solution)/shard_map/all_to_all | solution.py:79
  134.6 15.5 %copy-start.2 = (bf16[1,2,256,256]{3,2,1,0:T(8,128)(2,1)S(1)}, bf16[1,2,256,256]{3,2,1,0:T(8,128)(2,1)}, u32[]{:S(2)}) copy-start(bf16[1,2,256,256]{3,2,1,0:T(8,128)(2,1)} %param.16) | copy-start | bytes 786436
  134.6 15.5 %copy-start.4 = (bf16[2,256,256]{2,1,0:T(8,128)(2,1)S(1)}, bf16[2,256,256]{2,1,0:T(8,128)(2,1)}, u32[]{:S(2)}) copy-start(bf16[2,256,256]{2,1,0:T(8,128)(2,1)} %param.17) | copy-start | bytes 786436
  141.2 29.0 %all-to-all-start.1 = ((bf16[128,2,1,512]{3,1,2,0:T(2,128)(2,1)}), bf16[128,2,1,512]{3,1,2,0:T(2,128)(2,1)S(1)}, u32[]{:S(2)}, u32[]{:S(2)}) async-start(bf16[128,2,1,512]{3,1,2,0:T(2,128)(2,1)} %bitcast.152), calls=%async_computation.1 | async-start | bytes 524288 | tf_op jit(solution)/shard_map/all_to_all | solution.py:85
  150.1 34.3 %all-gather.11.cloned.1.call-start = ((), (), s32[]{:S(2)}) async-start(), calls=%async_computation.6 | async-start | bytes 1310720 | tf_op jit(solution)/shard_map/all_gather | solution.py:11
  151.6 66.8 %all-gather.13.cloned.1.call-start = ((), (), s32[]{:S(2)}) async-start(), calls=%async_computation.7 | async-start | bytes 1310720 | tf_op jit(solution)/shard_map/all_gather | solution.py:11
  218.4 8.6 %copy-start = (f32[256,256]{1,0:T(8,128)S(1)}, f32[256,256]{1,0:T(8,128)}, u32[]{:S(2)}) copy-start(f32[256,256]{1,0:T(8,128)} %fusion.89) | copy-start | bytes 786436
  230.3 37.0 %all-to-all-start.2 = ((bf16[1,2,128,512]{3,1,0,2:T(2,128)(2,1)}), bf16[1,2,128,512]{3,1,0,2:T(2,128)(2,1)S(1)}, u32[]{:S(2)}, u32[]{:S(2)}) async-start(bf16[1,2,128,512]{3,1,0,2:T(2,128)(2,1)} %copy.39), calls=%async_computation.2 | async-start | bytes 524288 | tf_op jit(solution)/shard_map/all_to_all | solution.py:97
Sparse Core Ops, SparseCore 0:
  14.0 34.8 all-gather.8
  51.1 32.0 all-gather.6
  153.0 31.3 all-gather.10
  186.3 32.0 all-gather.12
where the time goes:
time: 398 us; the launch traced here: 391 us
  waiting for transfers between devices  171 us (43%)
  other arithmetic  92.1 us (23%)
  starting transfers between devices  42.9 us (11%)
  matrix products  31 us (8%)
  blocking collectives  28.6 us (7%)
  between operations  14.2 us (4%)
  local copies, waits for them, and re-layouts  11.2 us (3%)
    all_gather x4, waiting for transfers between devices, prefix(): pieces = jax.tree.map(lambda part: lax.all_gather(part, axis), value)  113 us
    scatter-add x1, other arithmetic, per_device(): jax.ops.segment_sum(terms, targets, num_segments=arrived.shape[0])  81.1 us
    all_to_all x1, blocking collectives, per_device(): lax.all_to_all(sigma_rows.astype(jnp.bfloat16), 'energy', split_axis=0, c...  28.6 us
    all_to_all x1, waiting for transfers between devices, per_device(): lax.all_to_all(phonon_send, 'energy', split_axis=2, concat_axis=0, tiled=...  19.6 us
    all_to_all x1, waiting for transfers between devices, per_device(): lax.all_to_all(green_send, 'energy', split_axis=2, concat_axis=0, tiled=T...  19.5 us
    all_to_all x1, waiting for transfers between devices, per_device(): lax.all_to_all(pol_rows, 'energy', split_axis=0, concat_axis=2, tiled=True)  18.5 us
    all_to_all x1, starting transfers between devices, per_device(): lax.all_to_all(phonon_send, 'energy', split_axis=2, concat_axis=0, tiled=...  17.1 us
    all_to_all x1, starting transfers between devices, per_device(): lax.all_to_all(green_send, 'energy', split_axis=2, concat_axis=0, tiled=T...  16.8 us
  transfers between devices with their start and end apart: 7, of which 7 were waited for; matrix products, arithmetic and copies ran while one was open for 2% of the time, Pallas kernels for 0%

commit v1 on v0

v1 whole, which is shorter than its diff:
```python
import functools

import jax
import jax.numpy as jnp
from jax import lax
from jax.experimental import pallas as pl
from jax.experimental.pallas import tpu as pltpu
from jax.sharding import PartitionSpec as P

MESH = pl.DeviceIdType.MESH
F32 = jnp.float32
BF16 = jnp.bfloat16
NQ = 8


def dot(a, b, dims=((1,), (0,))):
    return lax.dot_general(a, b, (dims, ((), ())), preferred_element_type=F32)


def dot_t(a, b):
    return dot(a, b, ((1,), (1,)))


def split(value):
    high = value.astype(BF16)
    return high, (value - high.astype(F32)).astype(BF16)


def left_split(parts, right, product=dot):
    return product(parts[0], right) + product(parts[1], right)


def both_split(left, right, product=dot):
    return product(left[0], right[0]) + (product(left[0], right[1]) + product(left[1], right[0]))


def ones_where(condition, dtype=BF16):
    return jnp.where(condition, jnp.ones(condition.shape, F32), jnp.zeros(condition.shape, F32)).astype(dtype)


def kernel(
    nz, ny, order, pairs,
    g0e, hcoup, sigma_in, gph0, hph, pair_lo, freq_offset, pair_weight, active,
    out,
    state_out, state_in, zsrc, zdst, qsrc, qdst, perm, perm_t, hot, hot_t, weight_cols, lows, uppers,
    zsend, zrecv, qsend, qrecv, ysend, yrecv,
):
    energies = nz * NQ
    rz = order // nz
    rq = rz // NQ
    me = lax.axis_index("energy")
    y = lax.axis_index("slab")
    z = me // NQ
    q = me % NQ

    barrier = pltpu.get_barrier_semaphore()

    def greet_z(step, carry):
        there = ((z + step) % nz) * NQ + q
        pl.semaphore_signal(barrier, inc=1, device_id=(there, y), device_id_type=MESH)
        return carry

    def greet_q(step, carry):
        there = z * NQ + (q + step) % NQ
        pl.semaphore_signal(barrier, inc=1, device_id=(there, y), device_id_type=MESH)
        return carry

    lax.fori_loop(1, nz, greet_z, 0)
    lax.fori_loop(1, NQ, greet_q, 0)

    @pl.when(y > 0)
    def _():
        pl.semaphore_signal(barrier, inc=1, device_id=(me, y - 1), device_id_type=MESH)

    @pl.when(y < ny - 1)
    def _():
        pl.semaphore_signal(barrier, inc=1, device_id=(me, y + 1), device_id_type=MESH)

    def z_rows(place):
        return pl.ds(pl.multiple_of(place * rz, rz), rz)

    def q_rows(place):
        return pl.ds(pl.multiple_of(place * nz, nz), nz)

    def z_start(lane):
        source, target = zsrc.at[lane], zdst.at[lane]

        def send(distance):
            place = (z + distance) % nz
            pltpu.make_async_remote_copy(
                src_ref=source.at[z_rows(place)],
                dst_ref=target.at[z_rows(z)],
                send_sem=zsend.at[lane],
                recv_sem=zrecv.at[lane],
                device_id=(place * NQ + q, y),
                device_id_type=MESH,
            ).start()

        send(nz // 2)

        def both(step, carry):
            distance = nz // 2 - step
            send(distance)
            send(nz - distance)
            return carry

        lax.fori_loop(1, nz // 2, both, 0)
        target[z_rows(z)] = source[z_rows(z)]

    def z_wait(lane, sems):
        view = zdst.at[lane, pl.ds(0, order - rz)]
        pltpu.make_async_copy(view, view, sems.at[lane]).wait()

    def q_start(lane):
        source, target = qsrc.at[lane], qdst.at[lane]

        def send(step, carry):
            place = (q + step) % NQ
            pltpu.make_async_remote_copy(
                src_ref=source.at[q_rows(place)],
                dst_ref=target.at[q_rows(q)],
                send_sem=qsend.at[lane],
                recv_sem=qrecv.at[lane],
                device_id=(z * NQ + place, y),
                device_id_type=MESH,
            ).start()
            return carry

        lax.fori_loop(1, NQ, send, 0)
        target[q_rows(q)] = source[q_rows(q)]

    def q_wait(lane, sems):
        view = qdst.at[lane, pl.ds(0, energies - nz)]
        pltpu.make_async_copy(view, view, sems.at[lane]).wait()

    def y_copy(which):
        return pltpu.make_async_remote_copy(
            src_ref=state_out.at[which],
            dst_ref=state_in.at[which],
            send_sem=ysend.at[which],
            recv_sem=yrecv.at[which],
            device_id=(me, (y + 1) % ny),
            device_id_type=MESH,
        )

    def enter(which):
        @pl.when(y > 0)
        def _():
            y_copy(which).wait_recv()

        @pl.when(y == 0)
        def _():
            state_in[which] = jnp.zeros((order, order), BF16)

        return state_in[which]

    def leave(which, state):
        state_out[which] = state.astype(BF16)

        @pl.when(y < ny - 1)
        def _():
            y_copy(which).start()

    def to_q(z_lane, q_lane):
        z_wait(z_lane, zrecv)
        moved = dot(perm[...], zdst[z_lane]).astype(BF16)
        for row in range(rq):
            qsrc[q_lane, :, row * order : (row + 1) * order] = moved[row * energies : (row + 1) * energies]
        q_start(q_lane)

    def to_z(q_lane, z_lane):
        q_wait(q_lane, qrecv)
        rows = [qdst[q_lane, :, row * order : (row + 1) * order] for row in range(rq)]
        zsrc[z_lane] = dot(perm_t[...], jnp.concatenate(rows, axis=0)).astype(BF16)
        z_start(z_lane)

    transfers = [dot(g0e[0, slab], hcoup[slab]) for slab in range(2)]
    injected = [
        left_split(split(dot(g0e[0, slab], sigma_in[0, slab])), g0e[0, slab], dot_t) for slab in range(2)
    ]
    transfer_parts = [split(value) for value in transfers]
    injected_parts = split(injected[0])
    mapped = split(both_split(transfer_parts[1], transfer_parts[0]))
    carried = (
        both_split(split(both_split(transfer_parts[1], injected_parts)), transfer_parts[1], dot_t) + injected[1]
    )
    keep = jnp.where(active[0] > 0, 1.0, 0.0).astype(F32)

    neighbours = jnp.minimum(y, 1) + jnp.minimum(ny - 1 - y, 1)
    pl.semaphore_wait(barrier, (nz - 1) + (NQ - 1) + neighbours)

    entered = enter(0)
    last = both_split(split(left_split(mapped, entered)), mapped, dot_t) + carried
    leave(0, last)
    first = both_split(split(left_split(transfer_parts[0], entered)), transfer_parts[0], dot_t) + injected[0]
    zsrc[0] = (keep * first).astype(BF16)
    z_start(0)
    zsrc[1] = (keep * last).astype(BF16)
    z_start(1)

    row = lax.broadcasted_iota(jnp.int32, (order, order), 0)
    col = lax.broadcasted_iota(jnp.int32, (order, order), 1)

    def source_row(place):
        return (place % nz) * rz + rq * ((place // nz) % NQ) + place // energies

    perm[...] = ones_where(source_row(row) == col)
    perm_t[...] = ones_where(row == source_row(col))
    row = lax.broadcasted_iota(jnp.int32, (energies, energies), 0)
    col = lax.broadcasted_iota(jnp.int32, (energies, energies), 1)
    energy_of_row = ((row % nz) * NQ + row // nz).astype(F32)
    energy_of_col = ((col % nz) * NQ + col // nz).astype(F32)
    diagonal = row == col
    reorder = row == (col % nz) * NQ + col // nz

    def ordered(column):
        return jnp.sum(jnp.where(reorder, column, 0.0), axis=0, keepdims=True)

    def as_column(line):
        return jnp.sum(jnp.where(diagonal, line, 0.0), axis=1, keepdims=True)

    offsets = ordered(as_column(freq_offset[...].astype(F32)))
    for k in range(pairs):
        low = ordered(as_column(pair_lo[k : k + 1].astype(F32)))
        upper = low + offsets
        weight = as_column(ordered(as_column(pair_weight[k : k + 1])))
        hot[k] = ones_where(as_column(low) == energy_of_col)
        hot[pairs + k] = ones_where(as_column(upper) == energy_of_col)
        hot_t[k] = ones_where(low == energy_of_row)
        hot_t[pairs + k] = ones_where(upper == energy_of_row)
        weight_cols[k] = jnp.broadcast_to(weight, (energies, energies))

    ph_transfers = [split(dot(gph0[0, slab], hph[slab])) for slab in range(2)]

    def polarize(slab):
        q_wait(slab, qrecv)
        total = None
        for k in range(pairs):
            bottom = dot(hot[k], qdst[slab])
            top = dot(hot[pairs + k], qdst[slab])
            weight = weight_cols[k][:, :1]
            bottom = bottom * weight
            term = bottom * top
            total = term if total is None else total + term
            lows[slab, k] = bottom
            uppers[slab, k] = top * weight
        qsrc[2 + slab] = total.astype(BF16)
        q_start(2 + slab)

    to_q(0, 0)
    polarize(0)
    to_q(1, 1)
    to_z(2, 2)
    polarize(1)
    to_z(3, 3)

    def inject(slab):
        z_wait(2 + slab, zrecv)
        return left_split(split(dot(gph0[0, slab], zdst[2 + slab])), gph0[0, slab], dot_t)

    def carry_on(transfer, state_parts):
        return both_split(split(both_split(transfer, state_parts)), transfer, dot_t)

    entered = enter(1)
    before = both_split(split(left_split(ph_transfers[0], entered)), ph_transfers[0], dot_t)
    first = before + inject(0)
    zsrc[4] = first.astype(BF16)
    z_start(4)
    before = carry_on(ph_transfers[1], split(first))
    last = before + inject(1)
    zsrc[5] = last.astype(BF16)
    z_start(5)
    leave(1, last)

    def collect(slab):
        q_wait(4 + slab, qrecv)
        phonon = qdst[4 + slab].astype(F32)
        total = None
        for k in range(pairs):
            for table, others in ((k, uppers), (pairs + k, lows)):
                high, low = split(phonon * others[slab, k])
                term = dot(hot_t[table], high) + dot(hot_t[table], low)
                total = term if total is None else total + term
        qsrc[6 + slab] = total.astype(BF16)
        q_start(6 + slab)

    to_q(4, 4)
    collect(0)
    to_q(5, 5)
    to_z(6, 6)
    collect(1)
    to_z(7, 7)
    for slab in range(2):
        z_wait(6 + slab, zrecv)
        out[0, slab] = zdst[6 + slab]

    for lane in range(8):
        z_wait(lane, zsend)
        q_wait(lane, qsend)

    @pl.when(y < ny - 1)
    def _():
        for which in range(2):
            y_copy(which).wait_send()


def per_device(g0e, hcoup, sigma_in, gph0, hph, pair_lo, freq_offset, pair_weight, active):
    groups = lax.axis_size("energy")
    ny = lax.axis_size("slab")
    nz = groups // NQ
    order = g0e.shape[2]
    pairs = pair_lo.shape[1]
    lanes = (order // nz // NQ) * order
    vmem = pl.BlockSpec(memory_space=pltpu.VMEM)
    smem = pl.BlockSpec(memory_space=pltpu.SMEM)
    return pl.pallas_call(
        functools.partial(kernel, nz, ny, order, pairs),
        out_shape=jax.ShapeDtypeStruct(g0e.shape, BF16),
        in_specs=[vmem] * 8 + [smem],
        out_specs=vmem,
        scratch_shapes=[
            pltpu.VMEM((2, order, order), BF16),
            pltpu.VMEM((2, order, order), BF16),
            pltpu.VMEM((8, order, order), BF16),
            pltpu.VMEM((8, order, order), BF16),
            pltpu.VMEM((8, groups, lanes), BF16),
            pltpu.VMEM((8, groups, lanes), BF16),
            pltpu.VMEM((order, order), BF16),
            pltpu.VMEM((order, order), BF16),
            pltpu.VMEM((2 * pairs, groups, groups), BF16),
            pltpu.VMEM((2 * pairs, groups, groups), BF16),
            pltpu.VMEM((pairs, groups, groups), F32),
            pltpu.VMEM((2, pairs, groups, lanes), F32),
            pltpu.VMEM((2, pairs, groups, lanes), F32),
            pltpu.SemaphoreType.DMA((8,)),
            pltpu.SemaphoreType.DMA((8,)),
            pltpu.SemaphoreType.DMA((8,)),
            pltpu.SemaphoreType.DMA((8,)),
            pltpu.SemaphoreType.DMA((2,)),
            pltpu.SemaphoreType.DMA((2,)),
        ],
        compiler_params=pltpu.CompilerParams(
            collective_id=0, has_side_effects=True, vmem_limit_bytes=40 * 1024 * 1024
        ),
    )(g0e, hcoup, sigma_in, gph0, hph, pair_lo.T, freq_offset.reshape(1, -1), pair_weight.T, active)


def solution(mesh):
    placed = (
        P("energy", "slab", None, None),
        P("slab", None, None),
        P("energy", "slab", None, None),
        P("energy", "slab", None, None),
        P("slab", None, None),
        P(),
        P(),
        P(),
        P("energy"),
    )
    return jax.shard_map(
        per_device,
        mesh=mesh,
        in_specs=placed,
        out_specs=P("energy", "slab", None, None),
        check_vma=False,
    )
```

time: 398 us -> 110 us (0.28); the launches traced: 391 us -> 110 us
  waiting for transfers between devices: 171 us -> 0 us
  Pallas kernels: 0 us -> 103 us
  other arithmetic: 92.1 us -> 0 us
  starting transfers between devices: 42.9 us -> 0 us
  matrix products: 31 us -> 0 us
  blocking collectives: 28.6 us -> 0 us
  between operations: 14.2 us -> 0.69 us
  local copies, waits for them, and re-layouts: 11.2 us -> 6.13 us
    all_gather x4 -> x0, waiting for transfers between devices: 113 us -> none  [prefix(): pieces = jax.tree.map(lambda part: lax.all_gather(part, axis), value)]
    pallas_call x0 -> x1, Pallas kernels: none -> 103 us  [per_device(): pl.pallas_call(functools.partial(kernel, nz, ny, order, pairs), out_shape...]
    scatter-add x1 -> x0, other arithmetic: 81.1 us -> none  [per_device(): jax.ops.segment_sum(terms, targets, num_segments=arrived.shape[0])]
    all_to_all x3 -> x0, waiting for transfers between devices: 57.6 us -> none  [the longest x1 19.6 us: per_device(): lax.all_to_all(phonon_send, 'energy', split_axis=2, concat_axis=0, tiled=...]
    all_to_all x3 -> x0, starting transfers between devices: 42.7 us -> none  [the longest x1 17.1 us: per_device(): lax.all_to_all(phonon_send, 'energy', split_axis=2, concat_axis=0, tiled=...]
    dot_general x34 -> x0, matrix products: 31 us -> none  [the longest x14 15.1 us: sandwich(): return jnp.einsum('...ik,...lk->...il', left, outer, precision=precise)]
    all_to_all x1 -> x0, blocking collectives: 28.6 us -> none  [per_device(): lax.all_to_all(sigma_rows.astype(jnp.bfloat16), 'energy', split_axis=0, c...]
    gather x2 -> x0, local copies, waits for them, and re-layouts: 7.11 us -> none  [the longest x1 3.56 us: per_device(): upper_rows = arrived[top_idx].astype(jnp.float32)]
  transfers between devices with their start and end apart: 7 -> 0, of which waited for: 7 -> 0; matrix products, arithmetic and copies ran while one was open for 2% -> 0% of each run, Pallas kernels for 0% -> 0%
where the time goes in v1:
time: 110 us
  Pallas kernels  103 us (94%)
  local copies, waits for them, and re-layouts  6.13 us (6%)
    pallas_call x1, Pallas kernels, per_device(): pl.pallas_call(functools.partial(kernel, nz, ny, order, pairs), out_shape...  103 us
    unnamed x17, local copies, waits for them, and re-layouts  6.13 us

profile of v1, /device:TPU:24, one launch (start us, length us, event | category | flops | bytes accessed | tf_op | source)
XLA Modules:
  0.0 109.6 jit_solution(2561235367414719387)
XLA Ops:
  0.7 0.0 copy-start.6
  0.7 0.0 copy-start.5
  0.7 0.0 copy-start.7
  0.7 0.7 copy-done.6
  1.3 0.0 copy-done.5
  1.4 0.0 copy-done.7
  1.4 0.0 copy-start
  1.4 0.9 copy-done
  2.3 0.0 copy-start.1
  2.3 0.9 copy-done.1
  3.3 0.0 copy-start.2
  3.3 0.9 copy-done.2
  4.2 0.0 copy-start.3
  4.2 0.9 copy-done.3
  5.2 0.0 copy-start.4
  5.2 0.9 copy-done.4
  6.1 102.8 %shard_map.91 = bf16[1,2,256,256]{3,2,1,0:T(8,128)(2,1)S(1)} custom-call(bf16[1,2,256,256]{3,2,1,0:T(8,128)(2,1)S(1)} %copy-done, bf16[2,256,256]{2,1,0:T(8,128)(2,1)S(1)} %copy-done.1, bf16[1,2,256,256]{3,2,1,0:T(8,128)(2,1)S(1)} %copy-done.2, bf16[1,2,256,256]{3,2,1,0:T(8,128)(2,1)S(1)} %copy-done.3, bf16[2,256,256]{2,1,0:T(8,128)(2,1)S(1)} %copy-done.4, ...), custom_call_target="tpu_custom_call" | custom-call | tf_op jit(solution)/shard_map/pallas_call | solution.py:316
  108.9 0.7 copy.12
Async XLA Ops:
  0.7 0.7 copy-start.6
  0.7 0.7 copy-start.5
  0.7 0.7 copy-start.7
  1.4 1.0 copy-start
  2.3 0.9 copy-start.1
  3.3 0.9 copy-start.2
  4.2 0.9 copy-start.3
  5.2 0.9 copy-start.4

commit v2 on v1

v2 whole, which is shorter than its diff:
```python
import functools

import jax
import jax.numpy as jnp
from jax import lax
from jax.experimental import pallas as pl
from jax.experimental.pallas import tpu as pltpu
from jax.sharding import PartitionSpec as P

MESH = pl.DeviceIdType.MESH
F32 = jnp.float32
BF16 = jnp.bfloat16
TILE = (8, 128)


def dot(a, b, dims=((1,), (0,))):
    return lax.dot_general(a, b, (dims, ((), ())), preferred_element_type=F32)


def dot_t(a, b):
    return dot(a, b, ((1,), (1,)))


def split(value):
    high = value.astype(BF16)
    return high, (value - high.astype(F32)).astype(BF16)


def left_split(parts, right, product=dot):
    return product(parts[0], right) + product(parts[1], right)


def both_split(left, right, product=dot):
    return product(left[0], right[0]) + (product(left[0], right[1]) + product(left[1], right[0]))


def ones_where(condition, dtype=BF16):
    return jnp.where(condition, jnp.ones(condition.shape, F32), jnp.zeros(condition.shape, F32)).astype(dtype)


def kernel(
    nx, nz, ny, order, pairs,
    g0e_in, hcoup_in, sigma_source, gph0_in, hph_in, pair_lo_in, freq_offset_in, pair_weight_in, active_in,
    out,
    g0e, hcoup, sigma_in, gph0, hph, pair_lo, freq_offset, pair_weight, active,
    state_out, state_in, green_tiles, green_rows, pol_rows, pol_tiles, phonon_tiles, phonon_rows, sigma_rows, sigma_tiles,
    wide, entries, hot, hot_t, weight_cols, partners,
    insem, tsend, trecv, rsend, rrecv, ysend, yrecv,
):
    chips = nx * nz
    energies = 2 * chips
    rows, lanes = TILE
    bands = order // rows
    me = lax.axis_index("energy")
    y = lax.axis_index("slab")
    chip = me // 2
    core = me % 2
    z = chip // nx
    x = chip % nx

    inputs = [
        pltpu.make_async_copy(source, target, insem.at[index])
        for index, (source, target) in enumerate(
            [
                (g0e_in, g0e),
                (hcoup_in, hcoup),
                (sigma_source, sigma_in),
                (gph0_in, gph0),
                (hph_in, hph),
                (pair_lo_in, pair_lo),
                (freq_offset_in, freq_offset),
                (pair_weight_in, pair_weight),
                (active_in, active),
            ]
        )
    ]
    for copy in inputs:
        copy.start()

    barrier = pltpu.get_barrier_semaphore()

    def greet(step, carry):
        there = (me + step) % energies
        pl.semaphore_signal(barrier, inc=1, device_id=(there, y), device_id_type=MESH)
        return carry

    lax.fori_loop(1, energies, greet, 0)

    @pl.when(y > 0)
    def _():
        pl.semaphore_signal(barrier, inc=1, device_id=(me, y - 1), device_id_type=MESH)

    @pl.when(y < ny - 1)
    def _():
        pl.semaphore_signal(barrier, inc=1, device_id=(me, y + 1), device_id_type=MESH)

    def other_chips(send):
        def at_distance(distance):
            for beside in range(nx):
                send(((z + distance) % nz) * nx + (x + beside) % nx)

        at_distance(nz // 2)

        def both(step, carry):
            distance = nz // 2 - step
            for beside in range(nx):
                send(((z + distance) % nz) * nx + (x + beside) % nx)
                send(((z + nz - distance) % nz) * nx + (x + beside) % nx)
            return carry

        lax.fori_loop(1, nz // 2, both, 0)
        for beside in range(1, nx):
            send(z * nx + (x + beside) % nx)

    def tiles_start(stage, slab, source, target):
        def copy(there):
            return pltpu.make_async_remote_copy(
                src_ref=source.at[slab, there],
                dst_ref=target.at[me],
                send_sem=tsend.at[stage],
                recv_sem=trecv.at[stage],
                device_id=(2 * there + slab, y),
                device_id_type=MESH,
            )

        other_chips(lambda there: copy(there).start())

        @pl.when(core == slab)
        def _():
            pltpu.make_async_copy(source.at[slab, chip], target.at[me], trecv.at[stage]).start()

        @pl.when(core != slab)
        def _():
            copy(chip).start()

    def rows_start(stage, source, target):
        def copy(there):
            return pltpu.make_async_remote_copy(
                src_ref=source.at[there],
                dst_ref=target.at[core, chip],
                send_sem=rsend.at[stage],
                recv_sem=rrecv.at[stage, core],
                device_id=(there, y),
                device_id_type=MESH,
            )

        def both_cores(there):
            copy(2 * there + core).start()
            copy(2 * there + 1 - core).start()

        other_chips(both_cores)
        copy(2 * chip + 1 - core).start()
        pltpu.make_async_copy(source.at[me], target.at[core, chip], rrecv.at[stage, core]).start()

    def wait_bytes(view, sem):
        pltpu.make_async_copy(view, view, sem).wait()

    def y_copy(which):
        return pltpu.make_async_remote_copy(
            src_ref=state_out.at[which],
            dst_ref=state_in.at[which],
            send_sem=ysend.at[which],
            recv_sem=yrecv.at[which],
            device_id=(me, (y + 1) % ny),
            device_id_type=MESH,
        )

    def enter(which):
        @pl.when(y > 0)
        def _():
            y_copy(which).wait_recv()

        @pl.when(y == 0)
        def _():
            state_in[which] = jnp.zeros((order, order), BF16)

        return state_in[which]

    def leave(which, state):
        state_out[which] = state.astype(BF16)

        @pl.when(y < ny - 1)
        def _():
            y_copy(which).start()

    def to_tiles(value, target):
        for side in range(order // lanes):
            half = value[:, side * lanes : (side + 1) * lanes].reshape(bands, rows, lanes)
            target[side * bands : (side + 1) * bands] = half.astype(BF16)

    def from_tiles(source):
        halves = [
            source[side * bands : (side + 1) * bands].astype(F32).reshape(order, lanes) for side in range(order // lanes)
        ]
        return jnp.concatenate(halves, axis=1).astype(BF16)

    def spread(source):
        wide[...] = source[...].astype(F32).reshape(energies * rows, lanes)

    def line(row):
        return wide[pl.ds(row, energies, stride=rows), :]

    def gather_back(target):
        target[...] = wide[...].reshape(energies, rows, lanes).astype(BF16)

    for copy in inputs[:3]:
        copy.wait()
    transfers = [dot(g0e[0, slab], hcoup[slab]) for slab in range(2)]
    injected = [
        left_split(split(dot(g0e[0, slab], sigma_in[0, slab])), g0e[0, slab], dot_t) for slab in range(2)
    ]
    transfer_parts = [split(value) for value in transfers]
    injected_parts = split(injected[0])
    mapped = split(both_split(transfer_parts[1], transfer_parts[0]))
    carried = (
        both_split(split(both_split(transfer_parts[1], injected_parts)), transfer_parts[1], dot_t) + injected[1]
    )
    for copy in inputs[3:]:
        copy.wait()
    keep = jnp.where(active[0] > 0, 1.0, 0.0).astype(F32)

    pl.semaphore_wait(barrier, (energies - 1) + jnp.minimum(y, 1) + jnp.minimum(ny - 1 - y, 1))

    entered = enter(0)
    last = both_split(split(left_split(mapped, entered)), mapped, dot_t) + carried
    leave(0, last)
    first = both_split(split(left_split(transfer_parts[0], entered)), transfer_parts[0], dot_t) + injected[0]
    to_tiles(keep * first, green_tiles.at[0])
    tiles_start(0, 0, green_tiles, green_rows)
    to_tiles(keep * last, green_tiles.at[1])
    tiles_start(0, 1, green_tiles, green_rows)

    row = lax.broadcasted_iota(jnp.int32, (energies, energies), 0)
    col = lax.broadcasted_iota(jnp.int32, (energies, energies), 1)
    diagonal = row == col
    of_row = row.astype(F32)
    of_col = col.astype(F32)

    def as_column(values):
        return jnp.sum(jnp.where(diagonal, values, 0.0), axis=1, keepdims=True)

    offsets = freq_offset[...].astype(F32)
    for k in range(pairs):
        low = pair_lo[k : k + 1].astype(F32)
        upper = low + offsets
        hot[k] = ones_where(as_column(low) == of_col)
        hot[pairs + k] = ones_where(as_column(upper) == of_col)
        hot_t[k, :, :energies] = ones_where(low == of_row)
        hot_t[k, :, energies:] = ones_where(upper == of_row)
        weight_cols[k] = jnp.broadcast_to(as_column(pair_weight[k : k + 1]), (energies, energies))

    ph_transfers = [split(dot(gph0[0, slab], hph[slab])) for slab in range(2)]
    ph_mapped = split(both_split(ph_transfers[1], ph_transfers[0]))

    wait_bytes(green_rows, trecv.at[0])
    spread(green_rows)
    for entry in range(rows):
        entries[:, entry * lanes : (entry + 1) * lanes] = line(entry).astype(BF16)
    step = 2 * lanes
    for start in range(0, rows * lanes, step):
        part = entries[:, start : start + step]
        total = None
        for k in range(pairs):
            weight = weight_cols[k][:, :1]
            term = weight * dot(hot[k], part) * dot(hot[pairs + k], part)
            total = term if total is None else total + term
        for entry in range(2):
            wide[pl.ds(start // lanes + entry, energies, stride=rows), :] = total[:, entry * lanes : (entry + 1) * lanes]
    gather_back(pol_rows)
    rows_start(0, pol_rows, pol_tiles)

    for start in range(0, rows * lanes, step):
        part = entries[:, start : start + step]
        for k in range(pairs):
            weight = weight_cols[k][:, :1]
            partners[k, :energies, start : start + step] = weight * dot(hot[pairs + k], part)
            partners[k, energies:, start : start + step] = weight * dot(hot[k], part)

    def inject(slab):
        wait_bytes(pol_tiles.at[slab], rrecv.at[0, slab])
        return left_split(split(dot(gph0[0, slab], from_tiles(pol_tiles.at[slab]))), gph0[0, slab], dot_t)

    ph_injected = inject(0)
    ph_carried = both_split(split(both_split(ph_transfers[1], split(ph_injected))), ph_transfers[1], dot_t) + inject(1)
    entered = enter(1)
    last = both_split(split(left_split(ph_mapped, entered)), ph_mapped, dot_t) + ph_carried
    leave(1, last)
    first = both_split(split(left_split(ph_transfers[0], entered)), ph_transfers[0], dot_t) + ph_injected
    to_tiles(first, phonon_tiles.at[0])
    tiles_start(1, 0, phonon_tiles, phonon_rows)
    to_tiles(last, phonon_tiles.at[1])
    tiles_start(1, 1, phonon_tiles, phonon_rows)

    wait_bytes(phonon_rows, trecv.at[1])
    spread(phonon_rows)
    for start in range(0, rows * lanes, step):
        phonon = jnp.concatenate([line(start // lanes + entry) for entry in range(2)], axis=1)
        total = None
        for k in range(pairs):
            terms = [phonon * partners[k, side * energies : (side + 1) * energies, start : start + step] for side in range(2)]
            high, low = split(jnp.concatenate(terms, axis=0))
            term = dot(hot_t[k], high) + dot(hot_t[k], low)
            total = term if total is None else total + term
        for entry in range(2):
            wide[pl.ds(start // lanes + entry, energies, stride=rows), :] = total[:, entry * lanes : (entry + 1) * lanes]
    gather_back(sigma_rows)
    rows_start(1, sigma_rows, sigma_tiles)
    for slab in range(2):
        wait_bytes(sigma_tiles.at[slab], rrecv.at[1, slab])
        out[0, slab] = from_tiles(sigma_tiles.at[slab])

    for stage in range(2):
        wait_bytes(green_rows.at[pl.ds(0, energies - 1)], tsend.at[stage])
        wait_bytes(green_rows.at[pl.ds(0, energies - 1)], rsend.at[stage])

    @pl.when(y < ny - 1)
    def _():
        for which in range(2):
            y_copy(which).wait_send()


def per_device(nx, nz, g0e, hcoup, sigma_in, gph0, hph, pair_lo, freq_offset, pair_weight, active):
    energies = lax.axis_size("energy")
    ny = lax.axis_size("slab")
    order = g0e.shape[2]
    pairs = pair_lo.shape[1]
    rows, lanes = TILE
    operands = (g0e, hcoup, sigma_in, gph0, hph, pair_lo.T, freq_offset.reshape(1, -1), pair_weight.T, active)
    tiles = pltpu.VMEM((2, energies // 2, rows, lanes), BF16)
    lines = pltpu.VMEM((energies, rows, lanes), BF16)
    blocks = pltpu.VMEM((2, order, order), BF16)
    return pl.pallas_call(
        functools.partial(kernel, nx, nz, ny, order, pairs),
        out_shape=jax.ShapeDtypeStruct(g0e.shape, BF16),
        in_specs=[pl.BlockSpec(memory_space=pl.ANY)] * len(operands),
        out_specs=pl.BlockSpec(memory_space=pltpu.VMEM),
        scratch_shapes=[pltpu.VMEM(operand.shape, operand.dtype) for operand in operands[:-1]]
        + [
            pltpu.SMEM(active.shape, active.dtype),
            blocks,
            blocks,
            tiles,
            lines,
            lines,
            tiles,
            tiles,
            lines,
            lines,
            tiles,
            pltpu.VMEM((energies * rows, lanes), F32),
            pltpu.VMEM((energies, rows * lanes), BF16),
            pltpu.VMEM((2 * pairs, energies, energies), BF16),
            pltpu.VMEM((pairs, energies, 2 * energies), BF16),
            pltpu.VMEM((pairs, energies, energies), F32),
            pltpu.VMEM((pairs, 2 * energies, rows * lanes), F32),
            pltpu.SemaphoreType.DMA((len(operands),)),
            pltpu.SemaphoreType.DMA((2,)),
            pltpu.SemaphoreType.DMA((2,)),
            pltpu.SemaphoreType.DMA((2,)),
            pltpu.SemaphoreType.DMA((2, 2)),
            pltpu.SemaphoreType.DMA((2,)),
            pltpu.SemaphoreType.DMA((2,)),
        ],
        compiler_params=pltpu.CompilerParams(
            collective_id=0, has_side_effects=True, vmem_limit_bytes=56 * 1024 * 1024
        ),
    )(*operands)


def solution(mesh):
    placed = (
        P("energy", "slab", None, None),
        P("slab", None, None),
        P("energy", "slab", None, None),
        P("energy", "slab", None, None),
        P("slab", None, None),
        P(),
        P(),
        P(),
        P("energy"),
    )
    return jax.shard_map(
        functools.partial(per_device, 4, mesh.shape["energy"] // 8),
        mesh=mesh,
        in_specs=placed,
        out_specs=P("energy", "slab", None, None),
        check_vma=False,
    )
```

time: 110 us -> 92.5 us (0.84)
  Pallas kernels: 103 us -> 90 us
  local copies, waits for them, and re-layouts: 6.13 us -> 1.67 us
    pallas_call x1, Pallas kernels: 103 us -> 90 us  [per_device(): pl.pallas_call(functools.partial(kernel, nx, nz, ny, order, pairs), out_s...]
    unnamed x17 -> x1, local copies, waits for them, and re-layouts: 6.13 us -> 1.67 us
where the time goes in v2:
time: 92.5 us; the launch traced here: 92.3 us
  Pallas kernels  90 us (97%)
  local copies, waits for them, and re-layouts  1.67 us (2%)
    pallas_call x1, Pallas kernels, per_device(): pl.pallas_call(functools.partial(kernel, nx, nz, ny, order, pairs), out_s...  90 us

profile of v2, /device:TPU:24, one launch (start us, length us, event | category | flops | bytes accessed | tf_op | source)
XLA Modules:
  0.0 92.3 jit_solution(11571043062725601847)
XLA Ops:
  0.7 90.0 %shard_map.91 = bf16[1,2,256,256]{3,2,1,0:T(8,128)(2,1)} custom-call(bf16[1,2,256,256]{3,2,1,0:T(8,128)(2,1)} %g0e_in.1, bf16[2,256,256]{2,1,0:T(8,128)(2,1)} %hcoup_in.1, bf16[1,2,256,256]{3,2,1,0:T(8,128)(2,1)} %sigma_source.1, bf16[1,2,256,256]{3,2,1,0:T(8,128)(2,1)} %gph0_in.1, bf16[2,256,256]{2,1,0:T(8,128)(2,1)} %hph_in.1, s32[4,128]{1,0:T(4,128)} %bitcast.3, ...), custom_call_target="tpu_custom_call" | custom-call | tf_op jit(solution)/shard_map/pallas_call | solution.py:332
  90.6 1.7 %copy.12 = bf16[1,2,256,256]{3,2,1,0:T(8,128)(2,1)} copy(bf16[1,2,256,256]{3,2,1,0:T(8,128)(2,1)} %shard_map.91) | data formatting | bytes 524288

commit v3 on v2

--- a/solution.py
+++ b/solution.py
@@ -41,16 +41,16 @@
 def kernel(
     nx, nz, ny, order, pairs,
     g0e_in, hcoup_in, sigma_source, gph0_in, hph_in, pair_lo_in, freq_offset_in, pair_weight_in, active_in,
-    out,
+    sigma_tiles,
     g0e, hcoup, sigma_in, gph0, hph, pair_lo, freq_offset, pair_weight, active,
-    state_out, state_in, green_tiles, green_rows, pol_rows, pol_tiles, phonon_tiles, phonon_rows, sigma_rows, sigma_tiles,
+    state_out, state_in, held, lefts, green_tiles, green_rows, pol_rows, pol_tiles, phonon_tiles, phonon_rows, sigma_rows,
     wide, entries, hot, hot_t, weight_cols, partners,
     insem, tsend, trecv, rsend, rrecv, ysend, yrecv,
 ):
     chips = nx * nz
     energies = 2 * chips
     rows, lanes = TILE
-    bands = order // rows
+    bands, sides = order // rows, order // lanes
     me = lax.axis_index("energy")
     y = lax.axis_index("slab")
     chip = me // 2
@@ -84,7 +84,7 @@
         pl.semaphore_signal(barrier, inc=1, device_id=(there, y), device_id_type=MESH)
         return carry
 
-    lax.fori_loop(1, energies, greet, 0)
+    lax.fori_loop(1, energies, greet, 0, unroll=True)
 
     @pl.when(y > 0)
     def _():
@@ -112,12 +112,26 @@
         for beside in range(1, nx):
             send(z * nx + (x + beside) % nx)
 
+    def to_first_chips(send):
+        alone = 4
+
+        def at(step, carry):
+            turn = step - alone
+            shared = jnp.where(turn % 2 == 0, nz // 2 + turn // 2, alone + turn // 2)
+            place = jnp.where(jnp.logical_or(step < alone, step >= nz - alone), step, shared)
+            for beside in range(nx):
+                there = place * nx + (x + beside) % nx
+                pl.when(there != chip)(functools.partial(send, there))
+            return carry
+
+        lax.fori_loop(0, nz, at, 0)
+
     def tiles_start(stage, slab, source, target):
         def copy(there):
             return pltpu.make_async_remote_copy(
-                src_ref=source.at[slab, there],
+                src_ref=source.at[slab, there // sides, there % sides],
                 dst_ref=target.at[me],
-                send_sem=tsend.at[stage],
+                send_sem=tsend.at[stage, slab],
                 recv_sem=trecv.at[stage],
                 device_id=(2 * there + slab, y),
                 device_id_type=MESH,
@@ -127,17 +141,24 @@
 
         @pl.when(core == slab)
         def _():
-            pltpu.make_async_copy(source.at[slab, chip], target.at[me], trecv.at[stage]).start()
+            pltpu.make_async_copy(source.at[slab, chip // sides, chip % sides], target.at[me], trecv.at[stage]).start()
 
         @pl.when(core != slab)
         def _():
             copy(chip).start()
+
+    def tiles_sent(stage, slab):
+        wait_bytes(green_rows.at[pl.ds(0, chips - 1)], tsend.at[stage, slab])
+
+        @pl.when(core != slab)
+        def _():
+            wait_bytes(green_rows.at[0], tsend.at[stage, slab])
 
     def rows_start(stage, source, target):
         def copy(there):
             return pltpu.make_async_remote_copy(
                 src_ref=source.at[there],
-                dst_ref=target.at[core, chip],
+                dst_ref=target.at[core, chip // sides, chip % sides],
                 send_sem=rsend.at[stage],
                 recv_sem=rrecv.at[stage, core],
                 device_id=(there, y),
@@ -148,50 +169,85 @@
             copy(2 * there + core).start()
             copy(2 * there + 1 - core).start()
 
-        other_chips(both_cores)
+        (to_first_chips if stage else other_chips)(both_cores)
         copy(2 * chip + 1 - core).start()
-        pltpu.make_async_copy(source.at[me], target.at[core, chip], rrecv.at[stage, core]).start()
+        pltpu.make_async_copy(source.at[me], target.at[core, chip // sides, chip % sides], rrecv.at[stage, core]).start()
 
     def wait_bytes(view, sem):
         pltpu.make_async_copy(view, view, sem).wait()
 
-    def y_copy(which):
+    def y_copy(which, half):
         return pltpu.make_async_remote_copy(
-            src_ref=state_out.at[which],
-            dst_ref=state_in.at[which],
-            send_sem=ysend.at[which],
-            recv_sem=yrecv.at[which],
+            src_ref=state_out.at[which, half],
+            dst_ref=state_in.at[which, half],
+            send_sem=ysend.at[which, half],
+            recv_sem=yrecv.at[which, half],
             device_id=(me, (y + 1) % ny),
             device_id_type=MESH,
         )
 
-    def enter(which):
+    def pass_on(which, half, value):
+        held[1, half] = value
+        state_out[which, half] = value.astype(BF16)
+
+        @pl.when(y < ny - 1)
+        def _():
+            y_copy(which, half).start()
+
+    def half_rows(value, half):
+        return value[half * (order // 2) : (half + 1) * (order // 2)]
+
+    def chain(which, scale, composed, carried, transfer, injected, source, target):
+        @pl.when(y == 0)
+        def _():
+            for half in range(2):
+                pass_on(which, half, half_rows(carried, half))
+                held[0, half] = half_rows(injected, half)
+
+        def applied(parts, half):
+            return left_split([part[:, half * (order // 2) : (half + 1) * (order // 2)] for part in parts], state_in[which, half])
+
+        def later():
+            for half in range(2):
+                left = [half_rows(lefts[part], half) for part in range(2)]
+                pass_on(which, half, both_split(left, composed, dot_t) + half_rows(carried, half))
+
         @pl.when(y > 0)
         def _():
-            y_copy(which).wait_recv()
-
-        @pl.when(y == 0)
-        def _():
-            state_in[which] = jnp.zeros((order, order), BF16)
-
-        return state_in[which]
-
-    def leave(which, state):
-        state_out[which] = state.astype(BF16)
-
-        @pl.when(y < ny - 1)
-        def _():
-            y_copy(which).start()
+            y_copy(which, 0).wait_recv()
+            through, into = applied(composed, 0), applied(transfer, 0)
+            y_copy(which, 1).wait_recv()
+            lefts[0], lefts[1] = split(through + applied(composed, 1))
+            pl.when(y < ny - 1)(later)
+            first = both_split(split(into + applied(transfer, 1)), transfer, dot_t) + injected
+            for half in range(2):
+                held[0, half] = half_rows(first, half)
+
+        def go(slab):
+            if slab:
+                pl.when(y == ny - 1)(later)
+                tiles_sent(which, 0)
+            elif which:
+
+                @pl.when(y < ny - 1)
+                def _():
+                    for half in range(2):
+                        y_copy(which, half).wait_send()
+
+            value = jnp.concatenate([held[slab, 0], held[slab, 1]], axis=0)
+            to_tiles(value if scale is None else scale * value, source.at[slab])
+            tiles_start(which, slab, source, target)
+
+        go(0)
+        return lambda: go(1)
 
     def to_tiles(value, target):
-        for side in range(order // lanes):
+        for side in range(sides):
             half = value[:, side * lanes : (side + 1) * lanes].reshape(bands, rows, lanes)
-            target[side * bands : (side + 1) * bands] = half.astype(BF16)
+            target[:, side] = half.astype(BF16)
 
     def from_tiles(source):
-        halves = [
-            source[side * bands : (side + 1) * bands].astype(F32).reshape(order, lanes) for side in range(order // lanes)
-        ]
+        halves = [source[:, side].astype(F32).reshape(order, lanes) for side in range(sides)]
         return jnp.concatenate(halves, axis=1).astype(BF16)
 
     def spread(source):
@@ -221,14 +277,7 @@
 
     pl.semaphore_wait(barrier, (energies - 1) + jnp.minimum(y, 1) + jnp.minimum(ny - 1 - y, 1))
 
-    entered = enter(0)
-    last = both_split(split(left_split(mapped, entered)), mapped, dot_t) + carried
-    leave(0, last)
-    first = both_split(split(left_split(transfer_parts[0], entered)), transfer_parts[0], dot_t) + injected[0]
-    to_tiles(keep * first, green_tiles.at[0])
-    tiles_start(0, 0, green_tiles, green_rows)
-    to_tiles(keep * last, green_tiles.at[1])
-    tiles_start(0, 1, green_tiles, green_rows)
+    second_electrons = chain(0, keep, mapped, carried, transfer_parts[0], injected[0], green_tiles, green_rows)
 
     row = lax.broadcasted_iota(jnp.int32, (energies, energies), 0)
     col = lax.broadcasted_iota(jnp.int32, (energies, energies), 1)
@@ -251,6 +300,8 @@
 
     ph_transfers = [split(dot(gph0[0, slab], hph[slab])) for slab in range(2)]
     ph_mapped = split(both_split(ph_transfers[1], ph_transfers[0]))
+
+    second_electrons()
 
     wait_bytes(green_rows, trecv.at[0])
     spread(green_rows)
@@ -282,14 +333,7 @@
 
     ph_injected = inject(0)
     ph_carried = both_split(split(both_split(ph_transfers[1], split(ph_injected))), ph_transfers[1], dot_t) + inject(1)
-    entered = enter(1)
-    last = both_split(split(left_split(ph_mapped, entered)), ph_mapped, dot_t) + ph_carried
-    leave(1, last)
-    first = both_split(split(left_split(ph_transfers[0], entered)), ph_transfers[0], dot_t) + ph_injected
-    to_tiles(first, phonon_tiles.at[0])
-    tiles_start(1, 0, phonon_tiles, phonon_rows)
-    to_tiles(last, phonon_tiles.at[1])
-    tiles_start(1, 1, phonon_tiles, phonon_rows)
+    chain(1, None, ph_mapped, ph_carried, ph_transfers[0], ph_injected, phonon_tiles, phonon_rows)()
 
     wait_bytes(phonon_rows, trecv.at[1])
     spread(phonon_rows)
@@ -307,16 +351,15 @@
     rows_start(1, sigma_rows, sigma_tiles)
     for slab in range(2):
         wait_bytes(sigma_tiles.at[slab], rrecv.at[1, slab])
-        out[0, slab] = from_tiles(sigma_tiles.at[slab])
 
     for stage in range(2):
-        wait_bytes(green_rows.at[pl.ds(0, energies - 1)], tsend.at[stage])
+        tiles_sent(stage, 1)
         wait_bytes(green_rows.at[pl.ds(0, energies - 1)], rsend.at[stage])
 
     @pl.when(y < ny - 1)
     def _():
-        for which in range(2):
-            y_copy(which).wait_send()
+        for which, half in ((0, 0), (0, 1)):
+            y_copy(which, half).wait_send()
 
 
 def per_device(nx, nz, g0e, hcoup, sigma_in, gph0, hph, pair_lo, freq_offset, pair_weight, active):
@@ -326,12 +369,12 @@
     pairs = pair_lo.shape[1]
     rows, lanes = TILE
     operands = (g0e, hcoup, sigma_in, gph0, hph, pair_lo.T, freq_offset.reshape(1, -1), pair_weight.T, active)
-    tiles = pltpu.VMEM((2, energies // 2, rows, lanes), BF16)
+    tiles = pltpu.VMEM((2, order // rows, order // lanes, rows, lanes), BF16)
     lines = pltpu.VMEM((energies, rows, lanes), BF16)
-    blocks = pltpu.VMEM((2, order, order), BF16)
-    return pl.pallas_call(
+    blocks = pltpu.VMEM((2, 2, order // 2, order), BF16)
+    result = pl.pallas_call(
         functools.partial(kernel, nx, nz, ny, order, pairs),
-        out_shape=jax.ShapeDtypeStruct(g0e.shape, BF16),
+        out_shape=tiles,
         in_specs=[pl.BlockSpec(memory_space=pl.ANY)] * len(operands),
         out_specs=pl.BlockSpec(memory_space=pltpu.VMEM),
         scratch_shapes=[pltpu.VMEM(operand.shape, operand.dtype) for operand in operands[:-1]]
@@ -339,6 +382,8 @@
             pltpu.SMEM(active.shape, active.dtype),
             blocks,
             blocks,
+            pltpu.VMEM((2, 2, order // 2, order), F32),
+            pltpu.VMEM((2, order, order), BF16),
             tiles,
             lines,
             lines,
@@ -346,7 +391,6 @@
             tiles,
             lines,
             lines,
-            tiles,
             pltpu.VMEM((energies * rows, lanes), F32),
             pltpu.VMEM((energies, rows * lanes), BF16),
             pltpu.VMEM((2 * pairs, energies, energies), BF16),
@@ -354,17 +398,19 @@
             pltpu.VMEM((pairs, energies, energies), F32),
             pltpu.VMEM((pairs, 2 * energies, rows * lanes), F32),
             pltpu.SemaphoreType.DMA((len(operands),)),
-            pltpu.SemaphoreType.DMA((2,)),
+            pltpu.SemaphoreType.DMA((2, 2)),
             pltpu.SemaphoreType.DMA((2,)),
             pltpu.SemaphoreType.DMA((2,)),
             pltpu.SemaphoreType.DMA((2, 2)),
-            pltpu.SemaphoreType.DMA((2,)),
-            pltpu.SemaphoreType.DMA((2,)),
+            pltpu.SemaphoreType.DMA((2, 2)),
+            pltpu.SemaphoreType.DMA((2, 2)),
         ],
         compiler_params=pltpu.CompilerParams(
             collective_id=0, has_side_effects=True, vmem_limit_bytes=56 * 1024 * 1024
         ),
     )(*operands)
+    bands, sides = order // rows, order // lanes
+    return result.reshape(g0e.shape[:2] + (bands, sides, rows, lanes)).transpose(0, 1, 2, 4, 3, 5).reshape(g0e.shape)
 
 
 def solution(mesh):

time: 92.5 us -> 87.8 us (0.949)
  Pallas kernels: 90 us -> 86 us
  local copies, waits for them, and re-layouts: 1.67 us -> 0.71 us
    pallas_call x1, Pallas kernels: 90 us -> 86 us  [per_device(): pl.pallas_call(functools.partial(kernel, nx, nz, ny, order, pairs), out_s...]
    unnamed x1, local copies, waits for them, and re-layouts: 1.67 us -> 0.71 us
where the time goes in v3:
time: 87.8 us; the launch traced here: 87.3 us
  Pallas kernels  86 us (98%)
    pallas_call x1, Pallas kernels, per_device(): pl.pallas_call(functools.partial(kernel, nx, nz, ny, order, pairs), out_s...  86 us

profile of v3, /device:TPU:24, one launch (start us, length us, event | category | flops | bytes accessed | tf_op | source)
XLA Modules:
  0.0 87.3 jit_solution(11562246167622162995)
XLA Ops:
  0.7 86.0 %shard_map.91 = bf16[2,32,2,8,128]{4,3,2,1,0:T(8,128)(2,1)S(1)} custom-call(bf16[1,2,256,256]{3,2,1,0:T(8,128)(2,1)} %g0e_in.1, bf16[2,256,256]{2,1,0:T(8,128)(2,1)} %hcoup_in.1, bf16[1,2,256,256]{3,2,1,0:T(8,128)(2,1)} %sigma_source.1, bf16[1,2,256,256]{3,2,1,0:T(8,128)(2,1)} %gph0_in.1, bf16[2,256,256]{2,1,0:T(8,128)(2,1)} %hph_in.1, s32[4,128]{1,0:T(4,128)} %bitcast.9, ...), custom_call_target="tpu_custom_call" | custom-call | tf_op jit(solution)/shard_map/pallas_call | solution.py:375
  86.6 0.7 copy.11

commit v4 on v3

--- a/solution.py
+++ b/solution.py
@@ -84,8 +84,6 @@
         pl.semaphore_signal(barrier, inc=1, device_id=(there, y), device_id_type=MESH)
         return carry
 
-    lax.fori_loop(1, energies, greet, 0, unroll=True)
-
     @pl.when(y > 0)
     def _():
         pl.semaphore_signal(barrier, inc=1, device_id=(me, y - 1), device_id_type=MESH)
@@ -94,16 +92,24 @@
     def _():
         pl.semaphore_signal(barrier, inc=1, device_id=(me, y + 1), device_id_type=MESH)
 
+    def greet_far(turn, carry):
+        greet(energies // 2 + (turn + 1) // 2, 0)
+        greet(energies // 2 - (turn + 1) // 2, 0)
+        return carry
+
+    greet(energies // 2, 0)
+    lax.fori_loop(0, energies // 2 - 1, lambda turn, carry: greet_far(2 * turn + 1, carry), 0)
+
     def other_chips(send):
         def at_distance(distance):
-            for beside in range(nx):
+            for beside in sorted(range(nx), key=lambda step: -min(step, nx - step)):
                 send(((z + distance) % nz) * nx + (x + beside) % nx)
 
         at_distance(nz // 2)
 
         def both(step, carry):
             distance = nz // 2 - step
-            for beside in range(nx):
+            for beside in sorted(range(nx), key=lambda step: -min(step, nx - step)):
                 send(((z + distance) % nz) * nx + (x + beside) % nx)
                 send(((z + nz - distance) % nz) * nx + (x + beside) % nx)
             return carry
@@ -251,13 +257,13 @@
         return jnp.concatenate(halves, axis=1).astype(BF16)
 
     def spread(source):
-        wide[...] = source[...].astype(F32).reshape(energies * rows, lanes)
+        wide[: energies * rows] = source[...].astype(F32).reshape(energies * rows, lanes)
 
     def line(row):
         return wide[pl.ds(row, energies, stride=rows), :]
 
     def gather_back(target):
-        target[...] = wide[...].reshape(energies, rows, lanes).astype(BF16)
+        target[...] = wide[: energies * rows].reshape(energies, rows, lanes).astype(BF16)
 
     for copy in inputs[:3]:
         copy.wait()
@@ -294,8 +300,8 @@
         upper = low + offsets
         hot[k] = ones_where(as_column(low) == of_col)
         hot[pairs + k] = ones_where(as_column(upper) == of_col)
-        hot_t[k, :, :energies] = ones_where(low == of_row)
-        hot_t[k, :, energies:] = ones_where(upper == of_row)
+        hot_t[:, 2 * k * energies : (2 * k + 1) * energies] = ones_where(low == of_row)
+        hot_t[:, (2 * k + 1) * energies : (2 * k + 2) * energies] = ones_where(upper == of_row)
         weight_cols[k] = jnp.broadcast_to(as_column(pair_weight[k : k + 1]), (energies, energies))
 
     ph_transfers = [split(dot(gph0[0, slab], hph[slab])) for slab in range(2)]
@@ -339,12 +345,12 @@
     spread(phonon_rows)
     for start in range(0, rows * lanes, step):
         phonon = jnp.concatenate([line(start // lanes + entry) for entry in range(2)], axis=1)
-        total = None
-        for k in range(pairs):
-            terms = [phonon * partners[k, side * energies : (side + 1) * energies, start : start + step] for side in range(2)]
-            high, low = split(jnp.concatenate(terms, axis=0))
-            term = dot(hot_t[k], high) + dot(hot_t[k], low)
-            total = term if total is None else total + term
+        terms = [
+            (phonon * partners[k, side * energies : (side + 1) * energies, start : start + step]).astype(BF16)
+            for k in range(pairs)
+            for side in range(2)
+        ]
+        total = dot(hot_t[...], jnp.concatenate(terms, axis=0))
         for entry in range(2):
             wide[pl.ds(start // lanes + entry, energies, stride=rows), :] = total[:, entry * lanes : (entry + 1) * lanes]
     gather_back(sigma_rows)
@@ -391,10 +397,10 @@
             tiles,
             lines,
             lines,
-            pltpu.VMEM((energies * rows, lanes), F32),
+            pltpu.VMEM((energies * rows + rows, lanes), F32),
             pltpu.VMEM((energies, rows * lanes), BF16),
             pltpu.VMEM((2 * pairs, energies, energies), BF16),
-            pltpu.VMEM((pairs, energies, 2 * energies), BF16),
+            pltpu.VMEM((energies, 2 * pairs * energies), BF16),
             pltpu.VMEM((pairs, energies, energies), F32),
             pltpu.VMEM((pairs, 2 * energies, rows * lanes), F32),
             pltpu.SemaphoreType.DMA((len(operands),)),

time: 87.8 us -> 87 us (level)
  Pallas kernels: 86 us -> 84.8 us
    pallas_call x1, Pallas kernels: 86 us -> 84.8 us  [per_device(): pl.pallas_call(functools.partial(kernel, nx, nz, ny, order, pairs), out_s...]
where the time goes in v4:
time: 87 us; the launch traced here: 86.1 us
  Pallas kernels  84.8 us (97%)
    pallas_call x1, Pallas kernels, per_device(): pl.pallas_call(functools.partial(kernel, nx, nz, ny, order, pairs), out_s...  84.8 us

profile of v4, /device:TPU:24, one launch (start us, length us, event | category | flops | bytes accessed | tf_op | source)
XLA Modules:
  0.0 86.1 jit_solution(4200284356311713012)
XLA Ops:
  0.7 84.8 %shard_map.91 = bf16[2,32,2,8,128]{4,3,2,1,0:T(8,128)(2,1)S(1)} custom-call(bf16[1,2,256,256]{3,2,1,0:T(8,128)(2,1)} %g0e_in.1, bf16[2,256,256]{2,1,0:T(8,128)(2,1)} %hcoup_in.1, bf16[1,2,256,256]{3,2,1,0:T(8,128)(2,1)} %sigma_source.1, bf16[1,2,256,256]{3,2,1,0:T(8,128)(2,1)} %gph0_in.1, bf16[2,256,256]{2,1,0:T(8,128)(2,1)} %hph_in.1, s32[4,128]{1,0:T(4,128)} %bitcast.9, ...), custom_call_target="tpu_custom_call" | custom-call | tf_op jit(solution)/shard_map/pallas_call | solution.py:381
  85.4 0.7 copy.11
